TPU v7x, 32 devices: a whole 2x2x4 slice. The times are simulated.
32 devices in a mesh: row: 4 (over y, x), col: 8 (over z, core).
Axes of the slice: x: 2, y: 2, z: 4, core: 2. Of those that a mesh axis runs over, the one named last changes fastest.
Arguments:
- ancestor: float32 [24576, 24576], P('row', 'col'), may hold values from -6 to 6
- panels: float32 [4, 8, 256, 512], P(None, 'col'), may hold values from -0.125 to 0.125
- diag_inverse: float32 [4, 512, 512], P(None, 'row'), may hold values from -6 to 6
- fill_strips: int32 [4, 8], replicated, may hold values from 0 to 95, as said below
Outputs:
- upper_strips: float32 [4, 8, 256, 512], P(None, 'col')
- diagonal_blocks: float32 [4, 512, 512], P(None, 'row')
Inputs may be any that keep to these rules, and one draw needn't show every extreme that they name: `fill_strips`: each row lists 8 different strips in no particular order; of the strips s with the same s // 12 a row lists at most 2, and exactly 2 for some value; of the strips with the same s // 24 it lists at most 4, and exactly that many for some value.
All inputs are finite; a program needn't handle non-finite values.
Results may differ from a plain program's by a relative error of at most 0.0001.
Values sent between devices are 32-bit elements; how exact they have to be, the bound alone decides.
A program may use at most 192 MiB of HBM per device.

v0:
```python
import jax
import jax.numpy as jnp
from jax import lax
from jax.sharding import PartitionSpec as P


def local(ancestor, panels, diag_inverse, fill_strips):
    highest = lax.Precision.HIGHEST
    super_count = panels.shape[0]
    local_fill = panels.shape[1]
    strip_rows = panels.shape[2]
    panel_width = panels.shape[3]
    fill_count = fill_strips.shape[1]
    row_strips = ancestor.shape[0] // strip_rows
    col_strips = ancestor.shape[1] // strip_rows
    row_devices = lax.axis_size("row")
    col_devices = lax.axis_size("col")
    row_slots = 2 * local_fill * col_devices // row_devices
    col_slots = 2 * local_fill
    row_index = lax.axis_index("row")
    col_index = lax.axis_index("col")
    row_low = row_index * row_strips
    col_low = col_index * col_strips
    every_panel = lax.all_gather(panels, "col", axis=1, tiled=True)
    slot_products = []
    row_firsts = []
    ranks_all = []
    for supernode in range(super_count):
        listing = fill_strips[supernode]
        order = jnp.argsort(listing)
        sorted_list = listing[order]
        ranks = jnp.sum((listing[None, :] < listing[:, None]).astype(jnp.int32), axis=1)
        col_first = jnp.sum((sorted_list < col_low).astype(jnp.int32))
        row_first = jnp.sum((sorted_list < row_low).astype(jnp.int32))
        panel_parts = []
        col_starts = []
        for slot in range(col_slots):
            position = col_first + slot
            safe = jnp.clip(position, 0, fill_count - 1)
            strip = sorted_list[safe]
            valid = jnp.logical_and(
                position < fill_count,
                jnp.logical_and(strip >= col_low, strip < col_low + col_strips),
            )
            col_starts.append(jnp.clip(strip - col_low, 0, col_strips - 1) * strip_rows)
            piece = lax.dynamic_index_in_dim(every_panel[supernode], order[safe], 0, keepdims=False)
            panel_parts.append(piece * valid.astype(jnp.float32))
        stacked_panel = jnp.concatenate(panel_parts, axis=0)
        tiles = []
        for slot in range(row_slots):
            safe = jnp.clip(row_first + slot, 0, fill_count - 1)
            row_start = jnp.clip(sorted_list[safe] - row_low, 0, row_strips - 1) * strip_rows
            band = lax.dynamic_slice_in_dim(ancestor, row_start, strip_rows, 0)
            tiles.append(
                jnp.concatenate(
                    [lax.dynamic_slice_in_dim(band, start, strip_rows, 1) for start in col_starts],
                    axis=1,
                )
            )
        tile = jnp.concatenate(tiles, axis=0)
        product = jnp.dot(
            tile, stacked_panel, precision=highest, preferred_element_type=jnp.float32
        )
        slot_products.append(product.reshape(row_slots, strip_rows, panel_width))
        row_firsts.append(row_first)
        ranks_all.append(ranks)
    slot_totals = lax.psum(jnp.stack(slot_products), "col")
    picked = []
    for supernode in range(super_count):
        listing = fill_strips[supernode]
        position = col_index * local_fill + 0
        strip = listing[position]
        inside = jnp.logical_and(strip >= row_low, strip < row_low + row_strips)
        offset = jnp.clip(ranks_all[supernode][position] - row_firsts[supernode], 0, row_slots - 1)
        chosen = lax.dynamic_index_in_dim(slot_totals[supernode], offset, 0, keepdims=False)
        picked.append(chosen * inside.astype(jnp.float32))
    home_sums = jnp.stack(picked).reshape(super_count, local_fill, strip_rows, panel_width)
    totals = lax.psum(home_sums, "row")
    upper_strips = -totals
    diag_rows = diag_inverse.shape[1]
    left_part = lax.dynamic_slice_in_dim(panels, row_index * diag_rows, diag_rows, 3)
    diag_parts = jnp.einsum("kfrd,kfrw->kdw", left_part, upper_strips, precision=highest)
    summed = lax.psum(diag_parts, "col")
    return (upper_strips, diag_inverse - summed)


def solution(mesh):
    return jax.shard_map(
        local,
        mesh=mesh,
        in_specs=(P("row", "col"), P(None, "col", None, None), P(None, "row", None), P()),
        out_specs=(P(None, "col", None, None), P(None, "row", None)),
        check_vma=False,
    )
```

profile of v0, /device:TPU:1, one launch (start us, length us, event | category | flops | bytes accessed | tf_op | source)
XLA Modules:
  0.0 510.3 jit_solution(13184820010732681490)
XLA Ops:
  7.2 0.7 all-gather.2.cloned.1.call-update
  8.0 1.0 sort.59
  9.0 1.0 sort.60
  9.9 0.6 gather_fusion.1
  10.6 0.7 fusion.85
  16.0 0.7 fusion.102
  23.1 0.7 fusion.101
  26.3 1.0 sort.61
  27.2 1.0 sort.62
  28.2 0.6 gather_fusion.3
  28.8 0.7 fusion.89
  33.8 0.6 fusion.106
  40.7 0.6 fusion.105
  43.8 0.6 gather_fusion
  44.5 0.7 fusion.83
  49.6 0.7 fusion.100
  56.6 0.6 fusion.99
  59.7 0.6 gather_fusion.2
  60.3 0.7 fusion.87
  65.5 0.7 fusion.104
  72.5 0.6 fusion.103
  81.0 4.3 fusion.95
  85.3 6.4 %fusion.94 = (f32[256,256]{1,0:T(8,128)}, f32[256,256]{1,0:T(8,128)}, f32[256,256]{1,0:T(8,128)}, f32[256,256]{1,0:T(8,128)}, f32[256,256]{1,0:T(8,128)}, /*inde...) fusion(f32[6144,3072]{1,0:T(8,128)} %param.4, ...), kind=kLoop, calls=%fused_computation.141 | loop fusion | bytes 11010120 | tf_op jit(solution)/shard_map/dynamic_slice | solution.py:56
  91.7 71.6 %all-gather.2.cloned.1.call-done = f32[4,8,256,512]{3,2,1,0:T(8,128)} async-done(((f32[4,1,256,512]{3,2,1,0:T(8,128)}), f32[4,8,256,512]{3,2,1,0:T(8,128)}) %all-gather.2.cloned.1.call-update) | async-done | bytes 16777232 | tf_op jit(solution)/shard_map/all_gather | solution.py:24
  163.3 7.1 %fusion.96 = (f32[1,8,256,512]{3,2,1,0:T(8,128)S(1)}, f32[1,8,256,512]{3,2,1,0:T(8,128)S(1)}, f32[1,8,256,512]{3,2,1,0:T(8,128)S(1)}, f32[1,8,256,512]{3,2,1,0:T(8,128)S(1)}) fusion(f32[4,8,256,512]{3,2,1,0:T(8,128)} %all-gather.2.cloned.1.call-done), kind=kLoop, calls=%fused_computation.143 | loop fusion | bytes 33554432 | tf_op jit(solution)/shard_map/slice | solution.py:46
  170.4 0.1 multiply_bitcast_fusion.9
  170.9 0.7 copy-done.7
  172.1 3.4 fusion
  175.7 3.4 fusion.48
  179.2 3.4 fusion.16
  182.6 3.4 fusion.32
  186.1 4.2 pad_maximum_fusion
  190.3 0.6 constant_dynamic-slice_fusion.2
  193.5 0.6 constant_dynamic-slice_fusion
  196.7 0.2 convert_reduce_fusion.2
  197.0 0.6 dynamic_slice.345
  197.5 0.7 dynamic_slice.348
  198.2 0.2 convert_reduce_fusion
  198.4 0.6 dynamic_slice.351
  199.0 0.6 dynamic_slice.354
  204.7 159.0 %all-reduce.4.cloned.1.call-done = f32[4,4,256,512]{3,2,1,0:T(8,128)} async-done(((f32[4,4,256,512]{3,2,1,0:T(8,128)}), f32[4,4,256,512]{3,2,1,0:T(8,128)}) %all-reduce.4.cloned.1.call-update) | async-done | bytes 8388624 | tf_op jit(solution)/shard_map/psum | solution.py:67
  363.6 4.5 fusion.97
  368.3 1.5 maximum_bitcast_fusion
  369.9 70.0 %all-reduce.6.cloned.1.call-done = f32[4,1,256,512]{3,2,0,1:T(8,128)} async-done(((f32[4,1,256,512]{3,2,0,1:T(8,128)}), f32[4,1,256,512]{3,2,0,1:T(8,128)}) %all-reduce.6.cloned.1.call-update) | async-done | bytes 2097168 | tf_op jit(solution)/shard_map/psum | solution.py:78
  439.9 4.3 fusion.64
  444.3 1.7 negate_bitcast_fusion
  445.9 55.5 %all-reduce.8.cloned.1.call-done = f32[4,128,512]{2,1,0:T(8,128)} async-done(((f32[4,128,512]{2,1,0:T(8,128)}), f32[4,128,512]{2,1,0:T(8,128)}) %all-reduce.8.cloned.1.call-update) | async-done | bytes 1048592 | tf_op jit(solution)/shard_map/psum | solution.py:83
  501.4 2.4 sub.115
  (68 shorter events, 1.4 us)
Async XLA Ops:
  7.2 0.8 copy-start.21
  7.2 156.1 %all-gather.2.cloned.1.call-start = ((), (), s32[]{:S(2)}) async-start(), calls=%async_computation | async-start | bytes 18874368 | tf_op jit(solution)/shard_map/all_gather | solution.py:24
  7.9 355.7 %all-reduce.4.cloned.1.call-start = ((), (), s32[]{:S(2)}) async-start(), calls=%async_computation.1 | async-start | bytes 16777216 | tf_op jit(solution)/shard_map/psum | solution.py:67
  170.6 1.0 copy-start.7
  170.6 1.0 copy-start.8
  170.6 1.1 copy-start.9
  170.6 1.2 copy-start.10
  170.6 1.2 copy-start.11
  170.6 1.3 copy-start.12
  170.6 1.4 copy-start.13
  170.6 1.4 copy-start.20
  172.1 3.5 copy-start.14
  172.1 3.5 copy-start.15
  172.1 3.5 copy-start.16
  172.1 3.5 copy-start.17
  172.1 3.5 copy-start.18
  172.1 3.5 copy-start.19
  175.6 3.5 copy-start.2
  175.6 3.5 copy-start.3
  175.6 3.5 copy-start.4
  175.7 3.5 copy-start.5
  175.7 3.5 copy-start.6
  190.3 249.6 %all-reduce.6.cloned.1.call-start = ((), (), s32[]{:S(2)}) async-start(), calls=%async_computation.2 | async-start | bytes 4194304 | tf_op jit(solution)/shard_map/psum | solution.py:78
  369.9 131.5 %all-reduce.8.cloned.1.call-start = ((), (), s32[]{:S(2)}) async-start(), calls=%async_computation.3 | async-start | bytes 2097152 | tf_op jit(solution)/shard_map/psum | solution.py:83
  439.9 4.3 copy-start
  444.2 57.1 %copy-start.1 = (f32[4,128,512]{2,1,0:T(8,128)S(1)}, f32[4,128,512]{2,1,0:T(8,128)}, u32[]{:S(2)}) copy-start(f32[4,128,512]{2,1,0:T(8,128)} %param.6) | copy-start | bytes 3145732
Sparse Core Ops, SparseCore 0:
  9.6 153.6 all-gather.1
  190.4 173.1 all-reduce.3
  370.0 69.8 all-reduce.5
  444.4 56.9 all-reduce.7
where the time goes:
time: 514 us; the launch traced here: 510 us
  waiting for transfers between devices  357 us (69%)
  between operations  83 us (16%)
  local copies, waits for them, and re-layouts  35 us (7%)
  matrix products  18 us (4%)
  other arithmetic  17.4 us (3%)
    psum x1, waiting for transfers between devices, local(): slot_totals = lax.psum(jnp.stack(slot_products), 'col')  159 us
    all_gather x1, waiting for transfers between devices, local(): every_panel = lax.all_gather(panels, 'col', axis=1, tiled=True)  71.6 us
    psum x1, waiting for transfers between devices, local(): totals = lax.psum(home_sums, 'row')  70 us
    psum x1, waiting for transfers between devices, local(): summed = lax.psum(diag_parts, 'col')  55.5 us
    dot_general x4, matrix products, local(): jnp.dot(tile, stacked_panel, precision=highest, preferred_element_type=jn...  13.7 us
    dynamic_slice x2, local copies, waits for them, and re-layouts, local(): lax.dynamic_slice_in_dim(band, start, strip_rows, 1)  10.7 us
  transfers between devices with their start and end apart: 4, of which 4 were waited for; matrix products, arithmetic and copies ran while one was open for 6% of the time, Pallas kernels for 0%

commit v1 on v0

v1 whole, which is shorter than its diff:
```python
import functools

import jax
import jax.numpy as jnp
from jax import lax
from jax.experimental import pallas as pl
from jax.experimental.pallas import tpu as pltpu
from jax.sharding import PartitionSpec as P

MESH = pl.DeviceIdType.MESH


def split(x):
    high = x.astype(jnp.bfloat16)
    return high, (x - high.astype(jnp.float32)).astype(jnp.bfloat16)


def dot(a, b):
    return jnp.dot(a, b, preferred_element_type=jnp.float32)


def gather_kernel(row_slots, col_slots, strip, row_strips, col_strips,
                  fill_ref, ancestor, tiles, pick, rowq, starts_r, starts_c, sems):
    supers, fill = fill_ref.shape
    r, c = lax.axis_index("row"), lax.axis_index("col")
    mate = c + 1 - 2 * lax.rem(c, 2)
    slots = 2 * col_slots

    def one(k, carry):
        for s in range(2 * slots):
            pick[k, s] = 0
        for s in range(row_slots):
            starts_r[k, s] = 0
        for s in range(col_slots):
            starts_c[k, s] = 0
        values = [fill_ref[k, j] for j in range(fill)]
        for j in range(fill):
            s = values[j]
            in_row, in_col = s // row_strips, s // col_strips
            row_low, col_low = in_row * row_strips, in_col * col_strips
            row_slot, col_slot = jnp.int32(0), jnp.int32(0)
            for i in range(fill):
                if i != j:
                    less = values[i] < s
                    row_slot += jnp.where(less & (values[i] >= row_low), 1, 0)
                    col_slot += jnp.where(less & (values[i] >= col_low), 1, 0)
            rowq[k, j] = in_row * row_slots + row_slot

            @pl.when(in_row == r)
            def _():
                starts_r[k, row_slot] = s - row_low

            @pl.when(in_col == c)
            def _():
                starts_c[k, col_slot] = s - col_low
                pick[k, col_slot] = j
                pick[k, slots + col_slot] = 1

            @pl.when(in_col == mate)
            def _():
                pick[k, col_slots + col_slot] = j
                pick[k, slots + col_slots + col_slot] = 1

        for a in range(row_slots):
            for b in range(col_slots):
                copy_of(k, a, b).start()
        return carry

    def copy_of(k, a, b):
        row = pl.multiple_of(starts_r[k, a] * strip, strip)
        col = pl.multiple_of(starts_c[k, b] * strip, strip)
        return pltpu.make_async_copy(
            ancestor.at[pl.ds(row, strip), pl.ds(col, strip)],
            tiles.at[k, pl.ds(a * strip, strip), pl.ds(b * strip, strip)],
            sems.at[k, a, b],
        )

    lax.fori_loop(0, supers, one, 0)
    for k in range(supers):
        for a in range(row_slots):
            for b in range(col_slots):
                copy_of(k, a, b).wait()


def main_kernel(rows, cols, row_slots, col_slots,
                pick, rowq, tiles, panels, left, diag_inverse, upper, diag,
                own_tiles, mate_tiles, blocks, factor, factor_high, factor_low, product, by_row, dense, by_pair, final,
                terms, mate_terms, by_pair_diag, tile_sem,
                s_mate, r_mate, s_block, r_block, s_factor, r_factor, s_row, r_row, s_pair, r_pair, s_final, r_final,
                s_term, r_term, s_dpair, r_dpair, s_out, r_out):
    supers, _, strip, width = panels.shape
    waves = supers // 2
    pairs = cols // 2
    sub = strip // rows
    slots = 2 * col_slots
    diag_rows = diag_inverse.shape[1]
    chunk = diag_rows // pairs
    r, c = lax.axis_index("row"), lax.axis_index("col")
    core = lax.rem(c, 2)
    pair = c // 2
    mate = c + 1 - 2 * core
    sends = []

    def send(src, dst, ssem, rsem, row, col):
        copy = pltpu.make_async_remote_copy(
            src_ref=src, dst_ref=dst, send_sem=ssem, recv_sem=rsem, device_id=(row, col), device_id_type=MESH)
        copy.start()
        sends.append(copy)

    def arrive(dst, ssem, rsem):
        pltpu.make_async_remote_copy(
            src_ref=dst, dst_ref=dst, send_sem=ssem, recv_sem=rsem, device_id=(r, mate), device_id_type=MESH).wait_recv()

    def turn(value, step, size):
        return lax.rem(value + step, size)

    def rows_of(index, size):
        return pl.ds(pl.multiple_of(index * size, size), size)

    barrier = pltpu.get_barrier_semaphore()
    for d in range(1, cols):
        pl.semaphore_signal(barrier, inc=1, device_id=(r, turn(c, d, cols)), device_id_type=MESH)
    for d in range(1, rows):
        for col in (c, mate):
            pl.semaphore_signal(barrier, inc=1, device_id=(turn(r, d, rows), col), device_id_type=MESH)

    mine = rows_of(r, sub)
    own_copies = []
    for w in range(waves):
        copy = pltpu.make_async_copy(tiles.at[core * waves + w], own_tiles.at[w], tile_sem.at[w])
        copy.start()
        own_copies.append(copy)
    for w in range(waves):
        blocks[w][c] = panels[core * waves + w, 0, mine, :]

    pl.semaphore_wait(barrier, cols - 1 + 2 * (rows - 1))

    for w in range(waves):
        for d in range(1, cols):
            col = turn(c, d, cols)
            k = lax.rem(col, 2) * waves + w
            send(panels.at[k, 0, mine, :], blocks[w].at[c], s_block.at[w, d], r_block.at[w, c], r, col)
        send(tiles.at[(1 - core) * waves + w], mate_tiles.at[w], s_mate.at[w], r_mate.at[w], r, mate)

    for w in range(waves):
        k = core * waves + w
        for d in range(1, cols):
            source = turn(c, d, cols)
            arrive(blocks[w].at[source], s_block.at[w, d], r_block.at[w, source])
        for s in range(slots):
            factor[w, s, mine, :] = blocks[w][pick[k, s]] * pick[k, slots + s].astype(jnp.float32)
        for d in range(1, rows):
            part = factor.at[w, :, mine, :]
            send(part, part, s_factor.at[w, d], r_factor.at[w, r], turn(r, d, rows), c)

    half = col_slots * strip
    for w in range(waves):
        for d in range(1, rows):
            source = turn(r, d, rows)
            arrive(factor.at[w, :, rows_of(source, sub), :], s_factor.at[w, d], r_factor.at[w, source])
        for s in range(slots):
            high, low = split(factor[w, s])
            factor_high[pl.ds(s * strip, strip), :] = high
            factor_low[pl.ds(s * strip, strip), :] = low
        own_copies[w].wait()
        arrive(mate_tiles.at[w], s_mate.at[w], r_mate.at[w])

        def one(a, carry, w=w):
            band = rows_of(a, strip)
            total = None
            for first, held in ((0, own_tiles), (half, mate_tiles)):
                high, low = split(held[w, band, :])
                f_high = factor_high[pl.ds(first, half), :]
                f_low = factor_low[pl.ds(first, half), :]
                term = dot(high, f_low) + dot(low, f_high) + dot(high, f_high)
                total = term if total is None else total + term
            product[w, a] = total
            return carry

        lax.fori_loop(0, row_slots, one, 0)
        for d in range(1, rows):
            target = turn(r, d, rows)
            send(product.at[w, :, rows_of(target, sub), :], by_row[w].at[pl.ds(r * row_slots, row_slots)],
                 s_row.at[w, d], r_row.at[w, r], target, c)
        by_row[w][pl.ds(r * row_slots, row_slots)] = product[w, :, mine, :]

    for w in range(waves):
        k = core * waves + w
        for d in range(1, rows):
            source = turn(r, d, rows)
            arrive(by_row[w].at[pl.ds(source * row_slots, row_slots)], s_row.at[w, d], r_row.at[w, source])
        for j in range(cols):
            dense[w, j] = -by_row[w][rowq[k, j]]
        for d in range(1, pairs):
            target = turn(pair, d, pairs)
            send(dense.at[w, pl.ds(target * 2, 2)], by_pair.at[w, pair], s_pair.at[w, d], r_pair.at[w, pair],
                 r, target * 2 + core)
        by_pair[w, pair] = dense[w, pl.ds(pair * 2, 2)]

    for w in range(waves):
        k = core * waves + w
        for d in range(1, pairs):
            source = turn(pair, d, pairs)
            arrive(by_pair.at[w, source], s_pair.at[w, d], r_pair.at[w, source])
        total = by_pair[w, 0]
        for z in range(1, pairs):
            total += by_pair[w, z]
        final[w] = total
        for d in range(rows):
            target = turn(r, d, rows)
            for e in range(2):
                if d or e:
                    col = mate if e else c
                    send(final.at[w, lax.rem(col, 2)], upper.at[k, 0, mine, :],
                         s_final.at[w, d, e], r_final.at[w, r, core], target, col)
        upper[k, 0, mine, :] = final[w, core]

    for w in range(waves):
        for d in range(rows):
            source = turn(r, d, rows)
            for e in range(2):
                if d or e:
                    other = 1 - core if e else core
                    arrive(upper.at[other * waves + w, 0, rows_of(source, sub), :],
                           s_final.at[w, d, e], r_final.at[w, source, other])
        for e in range(2):
            k = e * waves + w
            l_high, l_low = split(left[k])
            u_high, u_low = split(upper[k, 0])
            terms[w, e] = dot(l_high, u_low) + dot(l_low, u_high) + dot(l_high, u_high)
        send(terms.at[w, 1 - core], mate_terms.at[w], s_term.at[w], r_term.at[w], r, mate)

    for w in range(waves):
        arrive(mate_terms.at[w], s_term.at[w], r_term.at[w])
        mate_terms[w] = mate_terms[w] + terms[w, core]
        for d in range(1, pairs):
            target = turn(pair, d, pairs)
            send(mate_terms.at[w, rows_of(target, chunk), :], by_pair_diag.at[w, pair],
                 s_dpair.at[w, d], r_dpair.at[w, pair], r, target * 2 + core)
        by_pair_diag[w, pair] = mate_terms[w, rows_of(pair, chunk), :]

    for w in range(waves):
        k = core * waves + w
        for d in range(1, pairs):
            source = turn(pair, d, pairs)
            arrive(by_pair_diag.at[w, source], s_dpair.at[w, d], r_dpair.at[w, source])
        total = by_pair_diag[w, 0]
        for z in range(1, pairs):
            total += by_pair_diag[w, z]
        place = rows_of(pair, chunk)
        diag[k, place, :] = diag_inverse[k, place, :] - total
        for d in range(1, cols):
            part = diag.at[k, place, :]
            send(part, part, s_out.at[w, d], r_out.at[w, c], r, turn(c, d, cols))

    for w in range(waves):
        for d in range(1, cols):
            source = turn(c, d, cols)
            k = lax.rem(source, 2) * waves + w
            arrive(diag.at[k, rows_of(source // 2, chunk), :], s_out.at[w, d], r_out.at[w, source])
    for copy in sends:
        copy.wait_send()


def local(ancestor, panels, diag_inverse, fill_strips):
    supers, local_fill, strip, width = panels.shape
    rows, cols = lax.axis_size("row"), lax.axis_size("col")
    fill = fill_strips.shape[1]
    row_slots = 2 * local_fill * cols // rows
    col_slots = 2 * local_fill
    row_strips, col_strips = ancestor.shape[0] // strip, ancestor.shape[1] // strip
    waves, pairs, sub, slots = supers // 2, cols // 2, strip // rows, 2 * col_slots
    diag_rows = diag_inverse.shape[1]
    chunk = diag_rows // pairs
    f32, i32, bf16 = jnp.float32, jnp.int32, jnp.bfloat16
    smem, vmem, anywhere = (pl.BlockSpec(memory_space=m) for m in (pltpu.SMEM, pltpu.VMEM, pl.ANY))
    dma = pltpu.SemaphoreType.DMA
    tiles, pick, rowq = pl.pallas_call(
        functools.partial(gather_kernel, row_slots, col_slots, strip, row_strips, col_strips),
        out_shape=(
            jax.ShapeDtypeStruct((supers, row_slots * strip, col_slots * strip), f32),
            jax.ShapeDtypeStruct((supers, 2 * slots), i32),
            jax.ShapeDtypeStruct((supers, fill), i32),
        ),
        in_specs=[smem, anywhere],
        out_specs=(anywhere, smem, smem),
        scratch_shapes=[
            pltpu.SMEM((supers, row_slots), i32),
            pltpu.SMEM((supers, col_slots), i32),
            dma((supers, row_slots, col_slots)),
        ],
        name="pick_tiles",
    )(fill_strips, ancestor)
    left = lax.dynamic_slice_in_dim(panels[:, 0], lax.axis_index("row") * diag_rows, diag_rows, 2)
    left = jnp.swapaxes(left, 1, 2)
    return pl.pallas_call(
        functools.partial(main_kernel, rows, cols, row_slots, col_slots),
        out_shape=(
            jax.ShapeDtypeStruct(panels.shape, f32),
            jax.ShapeDtypeStruct(diag_inverse.shape, f32),
        ),
        in_specs=[smem, smem, anywhere, vmem, vmem, vmem],
        out_specs=(vmem, vmem),
        scratch_shapes=[
            pltpu.VMEM((waves, row_slots * strip, col_slots * strip), f32),
            pltpu.VMEM((waves, row_slots * strip, col_slots * strip), f32),
            [pltpu.VMEM((cols, sub, width), f32)] * waves,
            pltpu.VMEM((waves, slots, strip, width), f32),
            pltpu.VMEM((slots * strip, width), bf16),
            pltpu.VMEM((slots * strip, width), bf16),
            pltpu.VMEM((waves, row_slots, strip, width), f32),
            [pltpu.VMEM((rows * row_slots, sub, width), f32)] * waves,
            pltpu.VMEM((waves, cols, sub, width), f32),
            pltpu.VMEM((waves, pairs, 2, sub, width), f32),
            pltpu.VMEM((waves, 2, sub, width), f32),
            pltpu.VMEM((waves, 2, diag_rows, width), f32),
            pltpu.VMEM((waves, diag_rows, width), f32),
            pltpu.VMEM((waves, pairs, chunk, width), f32),
            dma((waves,)),
            dma((waves,)), dma((waves,)),
            dma((waves, cols)), dma((waves, cols)),
            dma((waves, rows)), dma((waves, rows)),
            dma((waves, rows)), dma((waves, rows)),
            dma((waves, pairs)), dma((waves, pairs)),
            dma((waves, rows, 2)), dma((waves, rows, 2)),
            dma((waves,)), dma((waves,)),
            dma((waves, pairs)), dma((waves, pairs)),
            dma((waves, cols)), dma((waves, cols)),
        ],
        compiler_params=pltpu.CompilerParams(
            collective_id=0, has_side_effects=True, vmem_limit_bytes=56 * 2**20),
        name="update",
    )(pick, rowq, tiles, panels, left, diag_inverse)


def solution(mesh):
    return jax.shard_map(
        local,
        mesh=mesh,
        in_specs=(P("row", "col"), P(None, "col", None, None), P(None, "row", None), P()),
        out_specs=(P(None, "col", None, None), P(None, "row", None)),
        check_vma=False,
    )
```

time: 514 us -> 461 us (0.90)
  Pallas kernels: 0 us -> 450 us
  waiting for transfers between devices: 357 us -> 0 us
  between operations: 83 us -> 0.67 us
  local copies, waits for them, and re-layouts: 35 us -> 6.22 us
  matrix products: 18 us -> 0 us
  other arithmetic: 17.4 us -> 0 us
    pallas_call x0 -> x2, Pallas kernels: none -> 450 us  [the longest x1 257 us: local(): pl.pallas_call(functools.partial(gather_kernel, row_slots, col_slots, str...]
    psum x3 -> x0, waiting for transfers between devices: 284 us -> none  [the longest x1 159 us: local(): slot_totals = lax.psum(jnp.stack(slot_products), 'col')]
    all_gather x1 -> x0, waiting for transfers between devices: 71.6 us -> none  [local(): every_panel = lax.all_gather(panels, 'col', axis=1, tiled=True)]
    dot_general x5 -> x0, matrix products: 18 us -> none  [the longest x4 13.7 us: local(): jnp.dot(tile, stacked_panel, precision=highest, preferred_element_type=jn...]
    dynamic_slice x16 -> x2, local copies, waits for them, and re-layouts: 19.5 us -> 2.08 us  [local(): lax.dynamic_slice_in_dim(panels[:, 0], lax.axis_index('row') * diag_rows,...]
    slice x3 -> x0, local copies, waits for them, and re-layouts: 11.6 us -> none  [the longest x1 7.08 us: local(): every_panel[supernode]]
  transfers between devices with their start and end apart: 4 -> 0, of which waited for: 4 -> 0; matrix products, arithmetic and copies ran while one was open for 6% -> 0% of each run, Pallas kernels for 0% -> 0%
where the time goes in v1:
time: 461 us; the launch traced here: 457 us
  Pallas kernels  450 us (98%)
  local copies, waits for them, and re-layouts  6.22 us (1%)
    pallas_call x1, Pallas kernels, local(): pl.pallas_call(functools.partial(gather_kernel, row_slots, col_slots, str...  257 us
    pallas_call x1, Pallas kernels, local(): pl.pallas_call(functools.partial(main_kernel, rows, cols, row_slots, col_...  193 us

profile of v1, /device:TPU:1, one launch (start us, length us, event | category | flops | bytes accessed | tf_op | source)
XLA Modules:
  0.0 457.2 jit_solution(10238525725304749012)
XLA Ops:
  0.6 1.1 constant_dynamic-slice_fusion
  1.7 1.0 copy.6
  2.7 257.2 %pick_tiles.1 = (f32[4,1024,512]{2,1,0:T(8,128)}, s32[4,8]{1,0:T(4,128)}, s32[4,8]{1,0:T(4,128)}) custom-call(s32[4,8]{1,0:T(4,128)} %fill_ref.1, f32[6144,3072]{1,0:T(8,128)} %ancestor.1), custom_call_target="tpu_custom_call" | custom-call | tf_op jit(solution)/shard_map/pick_tiles/pallas_call | solution.py:278
  259.9 193.1 %update.1 = (f32[4,1,256,512]{3,2,1,0:T(8,128)}, f32[4,128,512]{2,1,0:T(8,128)}) custom-call(s32[4,8]{1,0:T(4,128)} %get-tuple-element.5.pick, s32[4,8]{1,0:T(4,128)} %get-tuple-element.6.rowq, f32[4,1024,512]{2,1,0:T(8,128)} %get-tuple-element.7.tiles, f32[4,1,256,512]{3,2,1,0:T(8,128)} %panels.1, f32[4,128,256]{2,1,0:T(8,128)} %bitcast.3, ...), custom_call_target="tpu_custom_call" | custom-call | tf_op jit(solution)/shard_map/update/pallas_call | solution.py:296
  453.1 0.0 copy-start
  453.1 3.2 copy.9
  456.2 0.0 copy-done
  456.2 1.0 copy.10
Async XLA Ops:
  453.1 3.2 copy-start

commit v2 on v1

--- a/solution.py
+++ b/solution.py
@@ -17,6 +17,10 @@
 
 def dot(a, b):
     return jnp.dot(a, b, preferred_element_type=jnp.float32)
+
+
+def dot_left(a, b):
+    return lax.dot_general(a, b, (((0,), (0,)), ((), ())), preferred_element_type=jnp.float32)
 
 
 def gather_kernel(row_slots, col_slots, strip, row_strips, col_strips,
@@ -82,14 +86,16 @@
                 copy_of(k, a, b).wait()
 
 
-def main_kernel(rows, cols, row_slots, col_slots,
+def main_kernel(rows, cols, halves, row_slots, col_slots,
                 pick, rowq, tiles, panels, left, diag_inverse, upper, diag,
                 own_tiles, mate_tiles, blocks, factor, factor_high, factor_low, product, by_row, dense, by_pair, final,
                 terms, mate_terms, by_pair_diag, tile_sem,
                 s_mate, r_mate, s_block, r_block, s_factor, r_factor, s_row, r_row, s_pair, r_pair, s_final, r_final,
-                s_term, r_term, s_dpair, r_dpair, s_out, r_out):
+                s_term, r_term, s_dpair, r_dpair, s_out, r_out, s_last, r_last):
     supers, _, strip, width = panels.shape
-    waves = supers // 2
+    held = supers // 2
+    waves = held * halves
+    part = width // halves
     pairs = cols // 2
     sub = strip // rows
     slots = 2 * col_slots
@@ -117,6 +123,9 @@
     def rows_of(index, size):
         return pl.ds(pl.multiple_of(index * size, size), size)
 
+    def which(w, of_core):
+        return of_core * held + w // halves, pl.ds((w % halves) * part, part)
+
     barrier = pltpu.get_barrier_semaphore()
     for d in range(1, cols):
         pl.semaphore_signal(barrier, inc=1, device_id=(r, turn(c, d, cols)), device_id_type=MESH)
@@ -126,35 +135,40 @@
 
     mine = rows_of(r, sub)
     own_copies = []
-    for w in range(waves):
-        copy = pltpu.make_async_copy(tiles.at[core * waves + w], own_tiles.at[w], tile_sem.at[w])
+    for i in range(held):
+        copy = pltpu.make_async_copy(tiles.at[core * held + i], own_tiles.at[i], tile_sem.at[i])
         copy.start()
         own_copies.append(copy)
     for w in range(waves):
-        blocks[w][c] = panels[core * waves + w, 0, mine, :]
+        k, lanes = which(w, core)
+        blocks[w][c] = panels[k, 0, mine, lanes]
 
     pl.semaphore_wait(barrier, cols - 1 + 2 * (rows - 1))
 
     for w in range(waves):
         for d in range(1, cols):
             col = turn(c, d, cols)
-            k = lax.rem(col, 2) * waves + w
-            send(panels.at[k, 0, mine, :], blocks[w].at[c], s_block.at[w, d], r_block.at[w, c], r, col)
-        send(tiles.at[(1 - core) * waves + w], mate_tiles.at[w], s_mate.at[w], r_mate.at[w], r, mate)
-
-    for w in range(waves):
-        k = core * waves + w
+            k, lanes = which(w, lax.rem(col, 2))
+            send(panels.at[k, 0, mine, lanes], blocks[w].at[c], s_block.at[w, d], r_block.at[w, c], r, col)
+        if w % halves == 0:
+            i = w // halves
+            send(tiles.at[(1 - core) * held + i], mate_tiles.at[i], s_mate.at[i], r_mate.at[i], r, mate)
+
+    def select(w):
+        k, _ = which(w, core)
         for d in range(1, cols):
             source = turn(c, d, cols)
             arrive(blocks[w].at[source], s_block.at[w, d], r_block.at[w, source])
         for s in range(slots):
             factor[w, s, mine, :] = blocks[w][pick[k, s]] * pick[k, slots + s].astype(jnp.float32)
         for d in range(1, rows):
-            part = factor.at[w, :, mine, :]
-            send(part, part, s_factor.at[w, d], r_factor.at[w, r], turn(r, d, rows), c)
+            share = factor.at[w, :, mine, :]
+            send(share, share, s_factor.at[w, d], r_factor.at[w, r], turn(r, d, rows), c)
 
     half = col_slots * strip
-    for w in range(waves):
+
+    def multiply(w):
+        i = w // halves
         for d in range(1, rows):
             source = turn(r, d, rows)
             arrive(factor.at[w, :, rows_of(source, sub), :], s_factor.at[w, d], r_factor.at[w, source])
@@ -162,14 +176,15 @@
             high, low = split(factor[w, s])
             factor_high[pl.ds(s * strip, strip), :] = high
             factor_low[pl.ds(s * strip, strip), :] = low
-        own_copies[w].wait()
-        arrive(mate_tiles.at[w], s_mate.at[w], r_mate.at[w])
-
-        def one(a, carry, w=w):
+        if w % halves == 0:
+            own_copies[i].wait()
+            arrive(mate_tiles.at[i], s_mate.at[i], r_mate.at[i])
+
+        def one(a, carry):
             band = rows_of(a, strip)
             total = None
-            for first, held in ((0, own_tiles), (half, mate_tiles)):
-                high, low = split(held[w, band, :])
+            for first, source in ((0, own_tiles), (half, mate_tiles)):
+                high, low = split(source[i, band, :])
                 f_high = factor_high[pl.ds(first, half), :]
                 f_low = factor_low[pl.ds(first, half), :]
                 term = dot(high, f_low) + dot(low, f_high) + dot(high, f_high)
@@ -184,8 +199,8 @@
                  s_row.at[w, d], r_row.at[w, r], target, c)
         by_row[w][pl.ds(r * row_slots, row_slots)] = product[w, :, mine, :]
 
-    for w in range(waves):
-        k = core * waves + w
+    def scatter(w):
+        k, _ = which(w, core)
         for d in range(1, rows):
             source = turn(r, d, rows)
             arrive(by_row[w].at[pl.ds(source * row_slots, row_slots)], s_row.at[w, d], r_row.at[w, source])
@@ -197,8 +212,8 @@
                  r, target * 2 + core)
         by_pair[w, pair] = dense[w, pl.ds(pair * 2, 2)]
 
-    for w in range(waves):
-        k = core * waves + w
+    def spread(w):
+        k, lanes = which(w, core)
         for d in range(1, pairs):
             source = turn(pair, d, pairs)
             arrive(by_pair.at[w, source], s_pair.at[w, d], r_pair.at[w, source])
@@ -211,26 +226,27 @@
             for e in range(2):
                 if d or e:
                     col = mate if e else c
-                    send(final.at[w, lax.rem(col, 2)], upper.at[k, 0, mine, :],
+                    send(final.at[w, lax.rem(col, 2)], upper.at[k, 0, mine, lanes],
                          s_final.at[w, d, e], r_final.at[w, r, core], target, col)
-        upper[k, 0, mine, :] = final[w, core]
-
-    for w in range(waves):
+        upper[k, 0, mine, lanes] = final[w, core]
+
+    def term_of(w):
         for d in range(rows):
             source = turn(r, d, rows)
             for e in range(2):
                 if d or e:
                     other = 1 - core if e else core
-                    arrive(upper.at[other * waves + w, 0, rows_of(source, sub), :],
+                    k, lanes = which(w, other)
+                    arrive(upper.at[k, 0, rows_of(source, sub), lanes],
                            s_final.at[w, d, e], r_final.at[w, source, other])
         for e in range(2):
-            k = e * waves + w
+            k, lanes = which(w, e)
             l_high, l_low = split(left[k])
-            u_high, u_low = split(upper[k, 0])
-            terms[w, e] = dot(l_high, u_low) + dot(l_low, u_high) + dot(l_high, u_high)
+            u_high, u_low = split(upper[k, 0, :, lanes])
+            terms[w, e] = dot_left(l_high, u_low) + dot_left(l_low, u_high) + dot_left(l_high, u_high)
         send(terms.at[w, 1 - core], mate_terms.at[w], s_term.at[w], r_term.at[w], r, mate)
 
-    for w in range(waves):
+    def term_scatter(w):
         arrive(mate_terms.at[w], s_term.at[w], r_term.at[w])
         mate_terms[w] = mate_terms[w] + terms[w, core]
         for d in range(1, pairs):
@@ -239,8 +255,8 @@
                  s_dpair.at[w, d], r_dpair.at[w, pair], r, target * 2 + core)
         by_pair_diag[w, pair] = mate_terms[w, rows_of(pair, chunk), :]
 
-    for w in range(waves):
-        k = core * waves + w
+    def term_spread(w):
+        k, lanes = which(w, core)
         for d in range(1, pairs):
             source = turn(pair, d, pairs)
             arrive(by_pair_diag.at[w, source], s_dpair.at[w, d], r_dpair.at[w, source])
@@ -248,16 +264,28 @@
         for z in range(1, pairs):
             total += by_pair_diag[w, z]
         place = rows_of(pair, chunk)
-        diag[k, place, :] = diag_inverse[k, place, :] - total
-        for d in range(1, cols):
-            part = diag.at[k, place, :]
-            send(part, part, s_out.at[w, d], r_out.at[w, c], r, turn(c, d, cols))
-
-    for w in range(waves):
-        for d in range(1, cols):
-            source = turn(c, d, cols)
-            k = lax.rem(source, 2) * waves + w
-            arrive(diag.at[k, rows_of(source // 2, chunk), :], s_out.at[w, d], r_out.at[w, source])
+        diag[k, place, lanes] = diag_inverse[k, place, lanes] - total
+        share = diag.at[k, place, lanes]
+        for d in range(1, pairs):
+            send(share, share, s_out.at[w, d], r_out.at[w, pair], r, turn(pair, d, pairs) * 2 + core)
+
+    def hand_over(w):
+        k, lanes = which(w, core)
+        for d in range(1, pairs):
+            source = turn(pair, d, pairs)
+            arrive(diag.at[k, rows_of(source, chunk), lanes], s_out.at[w, d], r_out.at[w, source])
+        share = diag.at[k, :, lanes]
+        send(share, share, s_last.at[w], r_last.at[w], r, mate)
+
+    def last(w):
+        k, lanes = which(w, 1 - core)
+        arrive(diag.at[k, :, lanes], s_last.at[w], r_last.at[w])
+
+    stages = (select, multiply, scatter, spread, term_of, term_scatter, term_spread, hand_over, last)
+    for step in range(waves + len(stages) - 1):
+        for index in reversed(range(len(stages))):
+            if 0 <= step - index < waves:
+                stages[index](step - index)
     for copy in sends:
         copy.wait_send()
 
@@ -269,7 +297,9 @@
     row_slots = 2 * local_fill * cols // rows
     col_slots = 2 * local_fill
     row_strips, col_strips = ancestor.shape[0] // strip, ancestor.shape[1] // strip
-    waves, pairs, sub, slots = supers // 2, cols // 2, strip // rows, 2 * col_slots
+    halves = 2 if width % 256 == 0 else 1
+    held, part = supers // 2, width // halves
+    waves, pairs, sub, slots = held * halves, cols // 2, strip // rows, 2 * col_slots
     diag_rows = diag_inverse.shape[1]
     chunk = diag_rows // pairs
     f32, i32, bf16 = jnp.float32, jnp.int32, jnp.bfloat16
@@ -283,18 +313,18 @@
             jax.ShapeDtypeStruct((supers, fill), i32),
         ),
         in_specs=[smem, anywhere],
-        out_specs=(anywhere, smem, smem),
+        out_specs=(vmem, smem, smem),
         scratch_shapes=[
             pltpu.SMEM((supers, row_slots), i32),
             pltpu.SMEM((supers, col_slots), i32),
             dma((supers, row_slots, col_slots)),
         ],
+        compiler_params=pltpu.CompilerParams(vmem_limit_bytes=56 * 2**20),
         name="pick_tiles",
     )(fill_strips, ancestor)
     left = lax.dynamic_slice_in_dim(panels[:, 0], lax.axis_index("row") * diag_rows, diag_rows, 2)
-    left = jnp.swapaxes(left, 1, 2)
     return pl.pallas_call(
-        functools.partial(main_kernel, rows, cols, row_slots, col_slots),
+        functools.partial(main_kernel, rows, cols, halves, row_slots, col_slots),
         out_shape=(
             jax.ShapeDtypeStruct(panels.shape, f32),
             jax.ShapeDtypeStruct(diag_inverse.shape, f32),
@@ -302,22 +332,22 @@
         in_specs=[smem, smem, anywhere, vmem, vmem, vmem],
         out_specs=(vmem, vmem),
         scratch_shapes=[
-            pltpu.VMEM((waves, row_slots * strip, col_slots * strip), f32),
-            pltpu.VMEM((waves, row_slots * strip, col_slots * strip), f32),
-            [pltpu.VMEM((cols, sub, width), f32)] * waves,
-            pltpu.VMEM((waves, slots, strip, width), f32),
-            pltpu.VMEM((slots * strip, width), bf16),
-            pltpu.VMEM((slots * strip, width), bf16),
-            pltpu.VMEM((waves, row_slots, strip, width), f32),
-            [pltpu.VMEM((rows * row_slots, sub, width), f32)] * waves,
-            pltpu.VMEM((waves, cols, sub, width), f32),
-            pltpu.VMEM((waves, pairs, 2, sub, width), f32),
-            pltpu.VMEM((waves, 2, sub, width), f32),
-            pltpu.VMEM((waves, 2, diag_rows, width), f32),
-            pltpu.VMEM((waves, diag_rows, width), f32),
-            pltpu.VMEM((waves, pairs, chunk, width), f32),
-            dma((waves,)),
-            dma((waves,)), dma((waves,)),
+            pltpu.VMEM((held, row_slots * strip, col_slots * strip), f32),
+            pltpu.VMEM((held, row_slots * strip, col_slots * strip), f32),
+            [pltpu.VMEM((cols, sub, part), f32)] * waves,
+            pltpu.VMEM((waves, slots, strip, part), f32),
+            pltpu.VMEM((slots * strip, part), bf16),
+            pltpu.VMEM((slots * strip, part), bf16),
+            pltpu.VMEM((waves, row_slots, strip, part), f32),
+            [pltpu.VMEM((rows * row_slots, sub, part), f32)] * waves,
+            pltpu.VMEM((waves, cols, sub, part), f32),
+            pltpu.VMEM((waves, pairs, 2, sub, part), f32),
+            pltpu.VMEM((waves, 2, sub, part), f32),
+            pltpu.VMEM((waves, 2, diag_rows, part), f32),
+            pltpu.VMEM((waves, diag_rows, part), f32),
+            pltpu.VMEM((waves, pairs, chunk, part), f32),
+            dma((held,)),
+            dma((held,)), dma((held,)),
             dma((waves, cols)), dma((waves, cols)),
             dma((waves, rows)), dma((waves, rows)),
             dma((waves, rows)), dma((waves, rows)),
@@ -325,7 +355,8 @@
             dma((waves, rows, 2)), dma((waves, rows, 2)),
             dma((waves,)), dma((waves,)),
             dma((waves, pairs)), dma((waves, pairs)),
-            dma((waves, cols)), dma((waves, cols)),
+            dma((waves, pairs)), dma((waves, pairs)),
+            dma((waves,)), dma((waves,)),
         ],
         compiler_params=pltpu.CompilerParams(
             collective_id=0, has_side_effects=True, vmem_limit_bytes=56 * 2**20),

time: 461 us -> 194 us (0.42)
  Pallas kernels: 450 us -> 184 us
    pallas_call x1, Pallas kernels: 257 us -> 10.1 us  [local(): pl.pallas_call(functools.partial(gather_kernel, row_slots, col_slots, str...]
    pallas_call x1, Pallas kernels: 193 us -> 174 us  [local(): pl.pallas_call(functools.partial(main_kernel, rows, cols, halves, row_slo...]
where the time goes in v2:
time: 194 us; the launch traced here: 191 us
  Pallas kernels  184 us (95%)
  local copies, waits for them, and re-layouts  6.02 us (3%)
    pallas_call x1, Pallas kernels, local(): pl.pallas_call(functools.partial(main_kernel, rows, cols, halves, row_slo...  174 us
    pallas_call x1, Pallas kernels, local(): pl.pallas_call(functools.partial(gather_kernel, row_slots, col_slots, str...  10.1 us
    unnamed x4, local copies, waits for them, and re-layouts  4.14 us

profile of v2, /device:TPU:1, one launch (start us, length us, event | category | flops | bytes accessed | tf_op | source)
XLA Modules:
  0.0 190.8 jit_solution(10158307541059448078)
XLA Ops:
  0.6 1.9 dynamic-slice_bitcast_fusion.left
  2.5 10.1 %pick_tiles.1 = (f32[4,1024,512]{2,1,0:T(8,128)}, s32[4,8]{1,0:T(4,128)}, s32[4,8]{1,0:T(4,128)}) custom-call(s32[4,8]{1,0:T(4,128)} %fill_ref.1, f32[6144,3072]{1,0:T(8,128)} %ancestor.1), custom_call_target="tpu_custom_call" | custom-call | tf_op jit(solution)/shard_map/pick_tiles/pallas_call | solution.py:308
  12.7 174.0 %update.1 = (f32[4,1,256,512]{3,2,1,0:T(8,128)}, f32[4,128,512]{2,1,0:T(8,128)}) custom-call(s32[4,8]{1,0:T(4,128)} %get-tuple-element.5.pick, s32[4,8]{1,0:T(4,128)} %get-tuple-element.6.rowq, f32[4,1024,512]{2,1,0:T(8,128)} %get-tuple-element.7.tiles, f32[4,1,256,512]{3,2,1,0:T(8,128)} %panels.1, f32[4,256,128]{2,1,0:T(8,128)} %dynamic-slice_bitcast_fusion.left, ...), custom_call_target="tpu_custom_call" | custom-call | tf_op jit(solution)/shard_map/update/pallas_call | solution.py:326
  186.7 0.0 copy-start
  186.7 3.2 %copy.8 = f32[4,1,256,512]{3,2,1,0:T(8,128)} copy(f32[4,1,256,512]{3,2,1,0:T(8,128)} %get-tuple-element.10) | data formatting | bytes 4194304
  189.9 0.0 copy-done
  189.9 1.0 copy.9
Async XLA Ops:
  186.7 3.2 %copy-start = (f32[4,128,512]{2,1,0:T(8,128)S(1)}, f32[4,128,512]{2,1,0:T(8,128)}, u32[]{:S(2)}) copy-start(f32[4,128,512]{2,1,0:T(8,128)} %get-tuple-element.11) | copy-start | bytes 3145732

commit v3 on v2

--- a/solution.py
+++ b/solution.py
@@ -88,7 +88,7 @@
 
 def main_kernel(rows, cols, halves, row_slots, col_slots,
                 pick, rowq, tiles, panels, left, diag_inverse, upper, diag,
-                own_tiles, mate_tiles, blocks, factor, factor_high, factor_low, product, by_row, dense, by_pair, final,
+                own_tiles, mate_tiles, blocks, factor, factor_both, product, by_row, dense, by_pair, final,
                 terms, mate_terms, by_pair_diag, tile_sem,
                 s_mate, r_mate, s_block, r_block, s_factor, r_factor, s_row, r_row, s_pair, r_pair, s_final, r_final,
                 s_term, r_term, s_dpair, r_dpair, s_out, r_out, s_last, r_last):
@@ -174,8 +174,8 @@
             arrive(factor.at[w, :, rows_of(source, sub), :], s_factor.at[w, d], r_factor.at[w, source])
         for s in range(slots):
             high, low = split(factor[w, s])
-            factor_high[pl.ds(s * strip, strip), :] = high
-            factor_low[pl.ds(s * strip, strip), :] = low
+            factor_both[pl.ds(s * strip, strip), pl.ds(0, part)] = high
+            factor_both[pl.ds(s * strip, strip), pl.ds(part, part)] = low
         if w % halves == 0:
             own_copies[i].wait()
             arrive(mate_tiles.at[i], s_mate.at[i], r_mate.at[i])
@@ -185,9 +185,8 @@
             total = None
             for first, source in ((0, own_tiles), (half, mate_tiles)):
                 high, low = split(source[i, band, :])
-                f_high = factor_high[pl.ds(first, half), :]
-                f_low = factor_low[pl.ds(first, half), :]
-                term = dot(high, f_low) + dot(low, f_high) + dot(high, f_high)
+                both = dot(high, factor_both[pl.ds(first, half), :])
+                term = both[:, part:] + dot(low, factor_both[pl.ds(first, half), pl.ds(0, part)]) + both[:, :part]
                 total = term if total is None else total + term
             product[w, a] = total
             return carry
@@ -281,11 +280,13 @@
         k, lanes = which(w, 1 - core)
         arrive(diag.at[k, :, lanes], s_last.at[w], r_last.at[w])
 
-    stages = (select, multiply, scatter, spread, term_of, term_scatter, term_spread, hand_over, last)
-    for step in range(waves + len(stages) - 1):
-        for index in reversed(range(len(stages))):
-            if 0 <= step - index < waves:
-                stages[index](step - index)
+    stages = ((select, 0, 52), (multiply, 32, 96), (scatter, 75, 141), (spread, 125, 167), (term_of, 156, 186),
+              (term_scatter, 166, 193), (term_spread, 174, 213), (hand_over, 192, 241), (last, 264, 293))
+    order = [
+        (first + (end - first) * w / max(1, waves - 1), stage, w) for stage, first, end in stages for w in range(waves)
+    ]
+    for _, stage, w in sorted(order, key=lambda item: item[0]):
+        stage(w)
     for copy in sends:
         copy.wait_send()
 
@@ -297,7 +298,7 @@
     row_slots = 2 * local_fill * cols // rows
     col_slots = 2 * local_fill
     row_strips, col_strips = ancestor.shape[0] // strip, ancestor.shape[1] // strip
-    halves = 2 if width % 256 == 0 else 1
+    halves = max(1, width // 128)
     held, part = supers // 2, width // halves
     waves, pairs, sub, slots = held * halves, cols // 2, strip // rows, 2 * col_slots
     diag_rows = diag_inverse.shape[1]
@@ -336,8 +337,7 @@
             pltpu.VMEM((held, row_slots * strip, col_slots * strip), f32),
             [pltpu.VMEM((cols, sub, part), f32)] * waves,
             pltpu.VMEM((waves, slots, strip, part), f32),
-            pltpu.VMEM((slots * strip, part), bf16),
-            pltpu.VMEM((slots * strip, part), bf16),
+            pltpu.VMEM((slots * strip, 2 * part), bf16),
             pltpu.VMEM((waves, row_slots, strip, part), f32),
             [pltpu.VMEM((rows * row_slots, sub, part), f32)] * waves,
             pltpu.VMEM((waves, cols, sub, part), f32),

time: 194 us -> 180 us (0.928); the launches traced: 191 us -> 180 us
  Pallas kernels: 184 us -> 173 us
    pallas_call x1, Pallas kernels: 174 us -> 163 us  [local(): pl.pallas_call(functools.partial(main_kernel, rows, cols, halves, row_slo...]
where the time goes in v3:
time: 180 us
  Pallas kernels  173 us (96%)
  local copies, waits for them, and re-layouts  6.02 us (3%)
    pallas_call x1, Pallas kernels, local(): pl.pallas_call(functools.partial(main_kernel, rows, cols, halves, row_slo...  163 us
    pallas_call x1, Pallas kernels, local(): pl.pallas_call(functools.partial(gather_kernel, row_slots, col_slots, str...  9.87 us
    unnamed x4, local copies, waits for them, and re-layouts  4.14 us

profile of v3, /device:TPU:1, one launch (start us, length us, event | category | flops | bytes accessed | tf_op | source)
XLA Modules:
  0.0 179.7 jit_solution(18235110778817351681)
XLA Ops:
  0.6 1.9 %dynamic-slice_bitcast_fusion.left = f32[4,256,128]{2,1,0:T(8,128)} fusion(f32[4,1,256,512]{3,2,1,0:T(8,128)} %panels.1, s32[]{:T(128)S(6)} %select_n.3), kind=kLoop, calls=%fused_computation | loop fusion | bytes 1048580 | tf_op jit(solution)/shard_map/dynamic_slice | solution.py:326
  2.5 9.9 %pick_tiles.1 = (f32[4,1024,512]{2,1,0:T(8,128)}, s32[4,8]{1,0:T(4,128)}, s32[4,8]{1,0:T(4,128)}) custom-call(s32[4,8]{1,0:T(4,128)} %fill_ref.1, f32[6144,3072]{1,0:T(8,128)} %ancestor.1), custom_call_target="tpu_custom_call" | custom-call | tf_op jit(solution)/shard_map/pick_tiles/pallas_call | solution.py:309
  12.4 163.1 %update.1 = (f32[4,1,256,512]{3,2,1,0:T(8,128)}, f32[4,128,512]{2,1,0:T(8,128)}) custom-call(s32[4,8]{1,0:T(4,128)} %get-tuple-element.5.pick, s32[4,8]{1,0:T(4,128)} %get-tuple-element.6.rowq, f32[4,1024,512]{2,1,0:T(8,128)} %get-tuple-element.7.tiles, f32[4,1,256,512]{3,2,1,0:T(8,128)} %panels.1, f32[4,256,128]{2,1,0:T(8,128)} %dynamic-slice_bitcast_fusion.left, ...), custom_call_target="tpu_custom_call" | custom-call | tf_op jit(solution)/shard_map/update/pallas_call | solution.py:327
  175.5 0.0 copy-start
  175.5 3.2 %copy.8 = f32[4,1,256,512]{3,2,1,0:T(8,128)} copy(f32[4,1,256,512]{3,2,1,0:T(8,128)} %get-tuple-element.10) | data formatting | bytes 4194304
  178.7 0.0 copy-done
  178.7 1.0 copy.9
Async XLA Ops:
  175.5 3.2 %copy-start = (f32[4,128,512]{2,1,0:T(8,128)S(1)}, f32[4,128,512]{2,1,0:T(8,128)}, u32[]{:S(2)}) copy-start(f32[4,128,512]{2,1,0:T(8,128)} %get-tuple-element.11) | copy-start | bytes 3145732

commit v4 on v3

--- a/solution.py
+++ b/solution.py
@@ -280,8 +280,8 @@
         k, lanes = which(w, 1 - core)
         arrive(diag.at[k, :, lanes], s_last.at[w], r_last.at[w])
 
-    stages = ((select, 0, 52), (multiply, 32, 96), (scatter, 75, 141), (spread, 125, 167), (term_of, 156, 186),
-              (term_scatter, 166, 193), (term_spread, 174, 213), (hand_over, 192, 241), (last, 264, 293))
+    stages = ((select, 0, 67), (multiply, 41, 87), (scatter, 72, 99), (spread, 83, 110), (term_of, 96, 132),
+              (term_scatter, 97, 133), (term_spread, 108, 153), (hand_over, 144, 220), (last, 147, 281))
     order = [
         (first + (end - first) * w / max(1, waves - 1), stage, w) for stage, first, end in stages for w in range(waves)
     ]
@@ -298,7 +298,7 @@
     row_slots = 2 * local_fill * cols // rows
     col_slots = 2 * local_fill
     row_strips, col_strips = ancestor.shape[0] // strip, ancestor.shape[1] // strip
-    halves = max(1, width // 128)
+    halves = max(1, width // 256)
     held, part = supers // 2, width // halves
     waves, pairs, sub, slots = held * halves, cols // 2, strip // rows, 2 * col_slots
     diag_rows = diag_inverse.shape[1]

time: 180 us -> 182 us (1.011)
  Pallas kernels: 173 us -> 175 us
where the time goes in v4:
time: 182 us
  Pallas kernels  175 us (96%)
  local copies, waits for them, and re-layouts  6.02 us (3%)
    pallas_call x1, Pallas kernels, local(): pl.pallas_call(functools.partial(main_kernel, rows, cols, halves, row_slo...  164 us
    pallas_call x1, Pallas kernels, local(): pl.pallas_call(functools.partial(gather_kernel, row_slots, col_slots, str...  10.8 us
    unnamed x4, local copies, waits for them, and re-layouts  4.14 us

profile of v4, /device:TPU:1, one launch (start us, length us, event | category | flops | bytes accessed | tf_op | source)
XLA Modules:
  0.0 181.7 jit_solution(15276607633325534155)
XLA Ops:
  0.6 1.9 %dynamic-slice_bitcast_fusion.left = f32[4,256,128]{2,1,0:T(8,128)} fusion(f32[4,1,256,512]{3,2,1,0:T(8,128)} %panels.1, s32[]{:T(128)S(6)} %select_n.3), kind=kLoop, calls=%fused_computation | loop fusion | bytes 1048580 | tf_op jit(solution)/shard_map/dynamic_slice | solution.py:326
  2.5 10.8 %pick_tiles.1 = (f32[4,1024,512]{2,1,0:T(8,128)}, s32[4,8]{1,0:T(4,128)}, s32[4,8]{1,0:T(4,128)}) custom-call(s32[4,8]{1,0:T(4,128)} %fill_ref.1, f32[6144,3072]{1,0:T(8,128)} %ancestor.1), custom_call_target="tpu_custom_call" | custom-call | tf_op jit(solution)/shard_map/pick_tiles/pallas_call | solution.py:309
  13.3 164.3 %update.1 = (f32[4,1,256,512]{3,2,1,0:T(8,128)}, f32[4,128,512]{2,1,0:T(8,128)}) custom-call(s32[4,8]{1,0:T(4,128)} %get-tuple-element.5.pick, s32[4,8]{1,0:T(4,128)} %get-tuple-element.6.rowq, f32[4,1024,512]{2,1,0:T(8,128)} %get-tuple-element.7.tiles, f32[4,1,256,512]{3,2,1,0:T(8,128)} %panels.1, f32[4,256,128]{2,1,0:T(8,128)} %dynamic-slice_bitcast_fusion.left, ...), custom_call_target="tpu_custom_call" | custom-call | tf_op jit(solution)/shard_map/update/pallas_call | solution.py:327
  177.6 0.0 copy-start
  177.6 3.2 %copy.8 = f32[4,1,256,512]{3,2,1,0:T(8,128)} copy(f32[4,1,256,512]{3,2,1,0:T(8,128)} %get-tuple-element.10) | data formatting | bytes 4194304
  180.8 0.0 copy-done
  180.8 1.0 copy.9
Async XLA Ops:
  177.6 3.2 %copy-start = (f32[4,128,512]{2,1,0:T(8,128)S(1)}, f32[4,128,512]{2,1,0:T(8,128)}, u32[]{:S(2)}) copy-start(f32[4,128,512]{2,1,0:T(8,128)} %get-tuple-element.11) | copy-start | bytes 3145732
